TPU v7x, 32 devices: a whole 2x2x4 slice. The times are simulated.
32 devices in a mesh: rows: 8 (over z, y), rhs: 4 (over x, core).
Axes of the slice: x: 2, y: 2, z: 4, core: 2. Of those that a mesh axis runs over, the one named last changes fastest.
Arguments:
- right_side: bfloat16 [64, 512, 256], P('rows', 'rhs'), may hold values from -6 to 6
- off_blocks: bfloat16 [64, 8, 256, 256], P('rows', None, 'rhs'), may hold values from -0.125 to 0.125
- diag_inverse: bfloat16 [64, 256, 256], P('rows', 'rhs'), may hold values from -0.375 to 0.375
- block_level: int32 [64], P('rows'), may hold values from 0 to 3, as said below
- block_columns: int32 [64, 8], P('rows'), may hold values from 0 to 63, as said below
Outputs:
- solved: bfloat16 [64, 512, 256], P('rows', 'rhs')
Inputs may be any that keep to these rules, and one draw needn't show every extreme that they name: `block_level`: among the 8 block rows of one index of rows every level occurs, none more than 4 times, and one level exactly 4 times. `block_columns`: block row i lies on index i // 8 of rows; each of its 8 block columns is a block row on the same index or one of the 3 indices below it (none below 0), of lower level when block row i has level 1 or more. Columns of one block row may repeat.
All inputs are finite; a program needn't handle non-finite values.
Results may differ from a plain program's by a relative error of at most 0.0075.
Values may be sent and summed in bfloat16 or wider, within the bound.
A program may use at most 128 MiB of HBM per device.

v0:
```python
import jax
import jax.numpy as jnp
from jax import lax
from jax.sharding import PartitionSpec as P

LEVELS = 4
REACH = 4


def shifted(block, axis, distance):
    devices = range(lax.axis_size(axis))
    route = [(i - distance, i) for i in devices if i - distance in devices]
    return lax.ppermute(block, axis, route)


def per_device(right_side, off_blocks, diag_inverse, block_level, block_columns):
    full_off, full_diag = (
        lax.all_gather(off_blocks, "rhs", axis=2, tiled=True),
        lax.all_gather(diag_inverse, "rhs", axis=1, tiled=True),
    )
    rows_here = block_level.shape[0]
    anchor = lax.axis_index("rows") * rows_here
    picked = jnp.zeros((rows_here, block_columns.shape[1]) + right_side.shape[1:], jnp.bfloat16)
    solved = jnp.zeros_like(right_side)
    source = right_side.astype(jnp.float32)
    for level_now in range(LEVELS):
        if level_now > 0:
            pieces = [solved]
            for distance in range(1, REACH):
                pieces.insert(0, shifted(solved, "rows", distance))
            window = jnp.concatenate(pieces, axis=0)
            begin_at = anchor - (REACH - 1) * rows_here
            offset = jnp.clip(block_columns - begin_at, 0, window.shape[0] - 1)
            picked = jnp.take(window, offset, axis=0)
            contribution = jnp.einsum(
                "ikrb,ikab->ira", picked, full_off, preferred_element_type=jnp.float32
            )
            residue = (source - contribution).astype(jnp.bfloat16)
        else:
            residue = right_side
        updated = jnp.einsum("irb,iab->ira", residue, full_diag, preferred_element_type=jnp.float32)
        solved = jnp.where(
            (block_level == level_now)[:, None, None], updated.astype(jnp.bfloat16), solved
        )
    return solved


def solution(mesh):
    return jax.shard_map(
        per_device,
        mesh=mesh,
        in_specs=(
            P("rows", "rhs", None),
            P("rows", None, "rhs", None),
            P("rows", "rhs", None),
            P("rows"),
            P("rows", None),
        ),
        out_specs=P("rows", "rhs", None),
        check_vma=False,
    )
```

profile of v0, /device:TPU:16, one launch (start us, length us, event | category | flops | bytes accessed | tf_op | source)
XLA Modules:
  0.0 224.3 jit_solution(675308023627332311)
XLA Ops:
  6.5 0.0 copy-start.5
  6.5 0.0 all-gather.3.cloned.1.call-start
  6.5 0.7 all-gather.3.cloned.1.call-update
  7.3 0.0 all-gather.5.cloned.1.call-start
  7.3 0.7 all-gather.5.cloned.1.call-update
  8.0 0.7 broadcast_compare_fusion.3
  8.7 18.1 %all-gather.3.cloned.1.call-done = bf16[8,256,256]{2,1,0:T(8,128)(2,1)} async-done(((bf16[8,64,256]{2,1,0:T(8,128)(2,1)}), bf16[8,256,256]{2,1,0:T(8,128)(2,1)}) %all-gather.3.cloned.1.call-update) | async-done | bytes 1048592 | tf_op jit(solution)/shard_map/all_gather | solution.py:19
  26.7 1.9 fusion.36
  28.6 4.3 %collective-permute-start = (bf16[8,128,256]{2,1,0:T(8,128)(2,1)S(1)}, bf16[8,128,256]{2,1,0:T(8,128)(2,1)S(1)}, u32[]{:S(2)}, u32[]{:S(2)}) collective-permute-start(bf16[8,128,256]{2,1,0:T(8,128)(2,1)S(1)} %fusion.36), channel_id=1, source_target_pairs={{0,12},{4,16},{8,20},{12,24},{16,28},{1,13},{5,17},{9,21},{13,25},... | collective-permute-start | bytes 1572872 | tf_op jit(solution)/shard_map/ppermute | solution.py:13
  32.9 1.9 collective-permute-start.1
  34.9 1.9 collective-permute-start.2
  36.8 0.0 copy-done.5
  36.8 0.1 reshape.39
  36.9 10.2 %collective-permute-done = bf16[8,128,256]{2,1,0:T(8,128)(2,1)S(1)} collective-permute-done((bf16[8,128,256]{2,1,0:T(8,128)(2,1)S(1)}, bf16[8,128,256]{2,1,0:T(8,128)(2,1)S(1)}, u32[]{:S(2)}, u32[]{:S(2)}) %collective-permute-start) | collective-permute-done | bytes 524320 | tf_op jit(solution)/shard_map/ppermute | solution.py:13
  47.1 9.7 %collective-permute-done.1 = bf16[8,128,256]{2,1,0:T(8,128)(2,1)S(1)} collective-permute-done((bf16[8,128,256]{2,1,0:T(8,128)(2,1)S(1)}, bf16[8,128,256]{2,1,0:T(8,128)(2,1)S(1)}, u32[]{:S(2)}, u32[]{:S(2)}) %collective-permute-start.1) | collective-permute-done | bytes 524320 | tf_op jit(solution)/shard_map/ppermute | solution.py:13
  56.8 0.0 copy-start.2
  56.8 0.8 copy-done.2
  57.6 22.7 %collective-permute-done.2 = bf16[8,128,256]{2,1,0:T(8,128)(2,1)} collective-permute-done((bf16[8,128,256]{2,1,0:T(8,128)(2,1)S(1)}, bf16[8,128,256]{2,1,0:T(8,128)(2,1)}, u32[]{:S(2)}, u32[]{:S(2)}) %collective-permute-start.2) | collective-permute-done | bytes 524320 | tf_op jit(solution)/shard_map/ppermute | solution.py:13
  80.2 1.5 pad_maximum_fusion
  81.7 0.0 copy-start.1
  81.7 2.8 %gather_fusion = bf16[64,128,256]{2,1,0:T(8,128)(2,1)} fusion(bf16[32,128,256]{2,1,0:T(8,128)(2,1)S(1)} %pad_maximum_fusion, s32[1024]{0:T(1024)S(1)} %pad_clamp_fusion), kind=kCustom, calls=%fused_computation.clone | custom fusion | bytes 8388864 | tf_op jit(solution)/shard_map/jit(_take)/gather | solution.py:34
  84.5 2.1 all-gather.5.cloned.1.call-done
  86.6 0.0 copy-done.1
  86.6 8.0 %fusion.37 = bf16[8,128,256]{2,1,0:T(8,128)(2,1)S(1)} fusion(bf16[8,128,256]{2,1,0:T(8,128)(2,1)S(1)} %fusion.36, bf16[8,256,256]{2,1,0:T(8,128)(2,1)} %all-gather.3.cloned.1.call-done, bf16[8,8,256,256]{3,2,1,0:T(8,128)(2,1)} %all-gather.5.cloned.1.call-done, bf16[8,8,128,256]{3,2,1,0:T(8,128)(2,1)} %bitcast.39, pred[8,8]{1,0:T(8,128)(4,1)S(1)} %get-tuple-element.6, ...), kind=kOutput, calls=%fused_computation.32 | convolution fusion | flops 1211367424 | bytes 15204424 | tf_op jit(solution)/shard_map/irb,iab->ira/dot_general | solution.py:41
  94.6 0.0 copy-start.4
  94.6 4.3 %collective-permute-start.3 = (bf16[8,128,256]{2,1,0:T(8,128)(2,1)S(1)}, bf16[8,128,256]{2,1,0:T(8,128)(2,1)S(1)}, u32[]{:S(2)}, u32[]{:S(2)}) collective-permute-start(bf16[8,128,256]{2,1,0:T(8,128)(2,1)S(1)} %fusion.37), channel_id=1, source_target_pairs={{0,12},{4,16},{8,20},{12,24},{16,28},{1,13},{5,17},{9,21},{13,25},... | collective-permute-start | bytes 1572872 | tf_op jit(solution)/shard_map/ppermute | solution.py:13
  98.9 1.9 collective-permute-start.4
  100.9 1.9 collective-permute-start.5
  102.8 10.3 %collective-permute-done.3 = bf16[8,128,256]{2,1,0:T(8,128)(2,1)S(1)} collective-permute-done((bf16[8,128,256]{2,1,0:T(8,128)(2,1)S(1)}, bf16[8,128,256]{2,1,0:T(8,128)(2,1)S(1)}, u32[]{:S(2)}, u32[]{:S(2)}) %collective-permute-start.3) | collective-permute-done | bytes 524320 | tf_op jit(solution)/shard_map/ppermute | solution.py:13
  113.1 9.7 %collective-permute-done.4 = bf16[8,128,256]{2,1,0:T(8,128)(2,1)S(1)} collective-permute-done((bf16[8,128,256]{2,1,0:T(8,128)(2,1)S(1)}, bf16[8,128,256]{2,1,0:T(8,128)(2,1)S(1)}, u32[]{:S(2)}, u32[]{:S(2)}) %collective-permute-start.4) | collective-permute-done | bytes 524320 | tf_op jit(solution)/shard_map/ppermute | solution.py:13
  122.8 23.4 %collective-permute-done.5 = bf16[8,128,256]{2,1,0:T(8,128)(2,1)S(1)} collective-permute-done((bf16[8,128,256]{2,1,0:T(8,128)(2,1)S(1)}, bf16[8,128,256]{2,1,0:T(8,128)(2,1)S(1)}, u32[]{:S(2)}, u32[]{:S(2)}) %collective-permute-start.5) | collective-permute-done | bytes 524320 | tf_op jit(solution)/shard_map/ppermute | solution.py:13
  146.2 0.0 copy-done.4
  146.2 0.3 pad_maximum_fusion.1
  146.4 0.0 copy-start
  146.4 2.8 %gather_fusion.1 = bf16[64,128,256]{2,1,0:T(8,128)(2,1)} fusion(bf16[32,128,256]{2,1,0:T(8,128)(2,1)S(1)} %pad_maximum_fusion.1, s32[1024]{0:T(1024)S(1)} %pad_clamp_fusion), kind=kCustom, calls=%fused_computation.1.clone | custom fusion | bytes 8388864 | tf_op jit(solution)/shard_map/jit(_take)/gather | solution.py:34
  149.2 0.0 copy-done
  149.2 8.0 %fusion.38 = bf16[8,128,256]{2,1,0:T(8,128)(2,1)S(1)} fusion(bf16[8,128,256]{2,1,0:T(8,128)(2,1)} %copy-done.4, bf16[8,256,256]{2,1,0:T(8,128)(2,1)S(1)} %copy-done, bf16[8,8,256,256]{3,2,1,0:T(8,128)(2,1)} %all-gather.5.cloned.1.call-done, bf16[8,8,128,256]{3,2,1,0:T(8,128)(2,1)} %bitcast.40, pred[8,8]{1,0:T(8,128)(4,1)S(1)} %get-tuple-element.6, ...), kind=kOutput, calls=%fused_computation.33 | convolution fusion | flops 1211367424 | bytes 15204424 | tf_op jit(solution)/shard_map/irb,iab->ira/dot_general | solution.py:41
  157.2 0.0 copy-start.3
  157.2 1.9 collective-permute-start.6
  159.1 1.9 collective-permute-start.7
  161.1 1.9 collective-permute-start.8
  163.0 12.7 %collective-permute-done.6 = bf16[8,128,256]{2,1,0:T(8,128)(2,1)S(1)} collective-permute-done((bf16[8,128,256]{2,1,0:T(8,128)(2,1)S(1)}, bf16[8,128,256]{2,1,0:T(8,128)(2,1)S(1)}, u32[]{:S(2)}, u32[]{:S(2)}) %collective-permute-start.6) | collective-permute-done | bytes 524320 | tf_op jit(solution)/shard_map/ppermute | solution.py:13
  175.7 6.3 %collective-permute-done.7 = bf16[8,128,256]{2,1,0:T(8,128)(2,1)S(1)} collective-permute-done((bf16[8,128,256]{2,1,0:T(8,128)(2,1)S(1)}, bf16[8,128,256]{2,1,0:T(8,128)(2,1)S(1)}, u32[]{:S(2)}, u32[]{:S(2)}) %collective-permute-start.7) | collective-permute-done | bytes 524320 | tf_op jit(solution)/shard_map/ppermute | solution.py:13
  182.1 0.0 copy-done.3
  182.1 22.5 %collective-permute-done.8 = bf16[8,128,256]{2,1,0:T(8,128)(2,1)S(1)} collective-permute-done((bf16[8,128,256]{2,1,0:T(8,128)(2,1)S(1)}, bf16[8,128,256]{2,1,0:T(8,128)(2,1)S(1)}, u32[]{:S(2)}, u32[]{:S(2)}) %collective-permute-start.8) | collective-permute-done | bytes 524320 | tf_op jit(solution)/shard_map/ppermute | solution.py:13
  204.6 1.3 pad_maximum_fusion.2
  205.9 2.8 %gather_fusion.2 = bf16[64,128,256]{2,1,0:T(8,128)(2,1)} fusion(bf16[32,128,256]{2,1,0:T(8,128)(2,1)S(1)} %pad_maximum_fusion.2, s32[1024]{0:T(1024)S(1)} %pad_clamp_fusion), kind=kCustom, calls=%fused_computation.2.clone | custom fusion | bytes 8388864 | tf_op jit(solution)/shard_map/jit(_take)/gather | solution.py:34
  208.7 8.7 %fusion.39 = bf16[8,128,256]{2,1,0:T(8,128)(2,1)} fusion(bf16[8,128,256]{2,1,0:T(8,128)(2,1)} %copy-done.3, bf16[8,256,256]{2,1,0:T(8,128)(2,1)S(1)} %copy-done, bf16[8,8,256,256]{3,2,1,0:T(8,128)(2,1)} %all-gather.5.cloned.1.call-done, bf16[8,8,128,256]{3,2,1,0:T(8,128)(2,1)} %bitcast.38, pred[8,8]{1,0:T(8,128)(4,1)S(1)} %get-tuple-element.6, ...), kind=kOutput, calls=%fused_computation.34 | convolution fusion | flops 1211367424 | bytes 15204424 | tf_op jit(solution)/shard_map/irb,iab->ira/dot_general | solution.py:41
  (2 shorter events, 0.0 us)
Async XLA Ops:
  6.5 30.3 %copy-start.5 = (s32[8,8]{1,0:T(8,128)S(1)}, s32[8,8]{1,0:T(8,128)}, u32[]{:S(2)}) copy-start(s32[8,8]{1,0:T(8,128)} %param.11) | copy-start | bytes 772
  6.5 20.2 %all-gather.3.cloned.1.call-start = ((), (), s32[]{:S(2)}) async-start(), calls=%async_computation | async-start | bytes 1310720 | tf_op jit(solution)/shard_map/all_gather | solution.py:19
  7.3 79.4 %all-gather.5.cloned.1.call-start = ((), (), s32[]{:S(2)}) async-start(), calls=%async_computation.1 | async-start | bytes 10485760 | tf_op jit(solution)/shard_map/all_gather | solution.py:18
  28.6 18.5 %collective-permute-start = (bf16[8,128,256]{2,1,0:T(8,128)(2,1)S(1)}, bf16[8,128,256]{2,1,0:T(8,128)(2,1)S(1)}, u32[]{:S(2)}, u32[]{:S(2)}) collective-permute-start(bf16[8,128,256]{2,1,0:T(8,128)(2,1)S(1)} %fusion.36), channel_id=1, source_target_pairs={{0,12},{4,16},{8,20},{12,24},{16,28},{1,13},{5,17},{9,21},{13,25},... | collective-permute-start | bytes 1572872 | tf_op jit(solution)/shard_map/ppermute | solution.py:13
  32.9 23.8 %collective-permute-start.1 = (bf16[8,128,256]{2,1,0:T(8,128)(2,1)S(1)}, bf16[8,128,256]{2,1,0:T(8,128)(2,1)S(1)}, u32[]{:S(2)}, u32[]{:S(2)}) collective-permute-start(bf16[8,128,256]{2,1,0:T(8,128)(2,1)S(1)} %fusion.36), channel_id=1, source_target_pairs={{0,8},{4,12},{8,16},{12,20},{16,24},{20,28},{1,9},{5,13},{9,17},{1... | collective-permute-start | bytes 1572872 | tf_op jit(solution)/shard_map/ppermute | solution.py:13
  34.9 45.4 %collective-permute-start.2 = (bf16[8,128,256]{2,1,0:T(8,128)(2,1)S(1)}, bf16[8,128,256]{2,1,0:T(8,128)(2,1)}, u32[]{:S(2)}, u32[]{:S(2)}) collective-permute-start(bf16[8,128,256]{2,1,0:T(8,128)(2,1)S(1)} %fusion.36), channel_id=1, source_target_pairs={{0,4},{4,8},{8,12},{12,16},{16,20},{20,24},{24,28},{1,5},{5,9},{9,... | collective-permute-start | bytes 1572872 | tf_op jit(solution)/shard_map/ppermute | solution.py:13
  56.8 0.8 copy-start.2
  81.7 4.9 %copy-start.1 = (bf16[8,128,256]{2,1,0:T(8,128)(2,1)S(1)}, bf16[8,128,256]{2,1,0:T(8,128)(2,1)}, u32[]{:S(2)}) copy-start(bf16[8,128,256]{2,1,0:T(8,128)(2,1)} %param.7) | copy-start | bytes 1572868
  94.6 51.5 %copy-start.4 = (bf16[8,128,256]{2,1,0:T(8,128)(2,1)}, bf16[8,128,256]{2,1,0:T(8,128)(2,1)S(1)}, u32[]{:S(2)}) copy-start(bf16[8,128,256]{2,1,0:T(8,128)(2,1)S(1)} %fusion.37) | copy-start | bytes 1572868
  94.6 18.5 %collective-permute-start.3 = (bf16[8,128,256]{2,1,0:T(8,128)(2,1)S(1)}, bf16[8,128,256]{2,1,0:T(8,128)(2,1)S(1)}, u32[]{:S(2)}, u32[]{:S(2)}) collective-permute-start(bf16[8,128,256]{2,1,0:T(8,128)(2,1)S(1)} %fusion.37), channel_id=1, source_target_pairs={{0,12},{4,16},{8,20},{12,24},{16,28},{1,13},{5,17},{9,21},{13,25},... | collective-permute-start | bytes 1572872 | tf_op jit(solution)/shard_map/ppermute | solution.py:13
  98.9 23.9 %collective-permute-start.4 = (bf16[8,128,256]{2,1,0:T(8,128)(2,1)S(1)}, bf16[8,128,256]{2,1,0:T(8,128)(2,1)S(1)}, u32[]{:S(2)}, u32[]{:S(2)}) collective-permute-start(bf16[8,128,256]{2,1,0:T(8,128)(2,1)S(1)} %fusion.37), channel_id=1, source_target_pairs={{0,8},{4,12},{8,16},{12,20},{16,24},{20,28},{1,9},{5,13},{9,17},{1... | collective-permute-start | bytes 1572872 | tf_op jit(solution)/shard_map/ppermute | solution.py:13
  100.9 45.3 %collective-permute-start.5 = (bf16[8,128,256]{2,1,0:T(8,128)(2,1)S(1)}, bf16[8,128,256]{2,1,0:T(8,128)(2,1)S(1)}, u32[]{:S(2)}, u32[]{:S(2)}) collective-permute-start(bf16[8,128,256]{2,1,0:T(8,128)(2,1)S(1)} %fusion.37), channel_id=1, source_target_pairs={{0,4},{4,8},{8,12},{12,16},{16,20},{20,24},{24,28},{1,5},{5,9},{9,... | collective-permute-start | bytes 1572872 | tf_op jit(solution)/shard_map/ppermute | solution.py:13
  146.4 2.8 %copy-start = (bf16[8,256,256]{2,1,0:T(8,128)(2,1)S(1)}, bf16[8,256,256]{2,1,0:T(8,128)(2,1)}, u32[]{:S(2)}) copy-start(bf16[8,256,256]{2,1,0:T(8,128)(2,1)} %all-gather.3.cloned.1.call-done) | copy-start | bytes 3145732
  157.2 24.9 %copy-start.3 = (bf16[8,128,256]{2,1,0:T(8,128)(2,1)}, bf16[8,128,256]{2,1,0:T(8,128)(2,1)S(1)}, u32[]{:S(2)}) copy-start(bf16[8,128,256]{2,1,0:T(8,128)(2,1)S(1)} %fusion.38) | copy-start | bytes 1572868
  157.2 18.5 %collective-permute-start.6 = (bf16[8,128,256]{2,1,0:T(8,128)(2,1)S(1)}, bf16[8,128,256]{2,1,0:T(8,128)(2,1)S(1)}, u32[]{:S(2)}, u32[]{:S(2)}) collective-permute-start(bf16[8,128,256]{2,1,0:T(8,128)(2,1)S(1)} %fusion.38), channel_id=1, source_target_pairs={{0,12},{4,16},{8,20},{12,24},{16,28},{1,13},{5,17},{9,21},{13,25},... | collective-permute-start | bytes 1572872 | tf_op jit(solution)/shard_map/ppermute | solution.py:13
  159.1 22.9 %collective-permute-start.7 = (bf16[8,128,256]{2,1,0:T(8,128)(2,1)S(1)}, bf16[8,128,256]{2,1,0:T(8,128)(2,1)S(1)}, u32[]{:S(2)}, u32[]{:S(2)}) collective-permute-start(bf16[8,128,256]{2,1,0:T(8,128)(2,1)S(1)} %fusion.38), channel_id=1, source_target_pairs={{0,8},{4,12},{8,16},{12,20},{16,24},{20,28},{1,9},{5,13},{9,17},{1... | collective-permute-start | bytes 1572872 | tf_op jit(solution)/shard_map/ppermute | solution.py:13
  161.1 43.5 %collective-permute-start.8 = (bf16[8,128,256]{2,1,0:T(8,128)(2,1)S(1)}, bf16[8,128,256]{2,1,0:T(8,128)(2,1)S(1)}, u32[]{:S(2)}, u32[]{:S(2)}) collective-permute-start(bf16[8,128,256]{2,1,0:T(8,128)(2,1)S(1)} %fusion.38), channel_id=1, source_target_pairs={{0,4},{4,8},{8,12},{12,16},{16,20},{20,24},{24,28},{1,5},{5,9},{9,... | collective-permute-start | bytes 1572872 | tf_op jit(solution)/shard_map/ppermute | solution.py:13
Sparse Core Ops, SparseCore 0:
  8.9 17.7 all-gather.2
  28.3 58.2 all-gather.4
where the time goes:
time: 225 us; the launch traced here: 224 us
  waiting for transfers between devices  149 us (66%)
  matrix products  26.5 us (12%)
  starting transfers between devices  22.1 us (10%)
  between operations  13.6 us (6%)
  local copies, waits for them, and re-layouts  9.27 us (4%)
  other arithmetic  3.71 us (2%)
    ppermute x9, waiting for transfers between devices, shifted(): return lax.ppermute(block, axis, route)  127 us
    dot_general x4, matrix products, per_device(): jnp.einsum('irb,iab->ira', residue, full_diag, preferred_element_type=jnp...  26.5 us
    ppermute x9, starting transfers between devices, shifted(): return lax.ppermute(block, axis, route)  22.1 us
    all_gather x1, waiting for transfers between devices, per_device(): lax.all_gather(diag_inverse, 'rhs', axis=1, tiled=True)  18.1 us
    gather x3, local copies, waits for them, and re-layouts, per_device(): picked = jnp.take(window, offset, axis=0)  8.37 us
  transfers between devices with their start and end apart: 11, of which 11 were waited for; matrix products, arithmetic and copies ran while one was open for 3% of the time, Pallas kernels for 0%

commit v1 on v0

v1 whole, which is shorter than its diff:
```python
import functools

import jax
import jax.numpy as jnp
from jax import lax
from jax.experimental import pallas as pl
from jax.experimental.pallas import tpu as pltpu
from jax.sharding import PartitionSpec as P

REACH = 4
BELOW = REACH - 1
MESH = pl.DeviceIdType.MESH
FIRST = (0, 1, 2, 4)
LAST = (3, 5, 6, 7)
AHEAD = 3


def nt(a, b):
    return lax.dot_general(a, b, (((1,), (1,)), ((), ())), preferred_element_type=jnp.float32)


def kernel(
    n, level_ref, cols_ref, lvl_ref, right_ref, off_ref, diag_ref, out_ref,
    fac, inv, win, land0, land1, land2, sol0, sol1, sol2, fin, lvl_in, lvl_s, rank, perm, lev,
    lvl_send, lvl_recv, lvl_sem, x_send, x_recv, c_send, c_recv, f_send, f_recv,
    w0_send, w0_recv, w1_send, w1_recv, w2_send, w2_recv,
):
    rows, kk, part, bs = off_ref.shape
    me, mine = lax.axis_index("rows"), lax.axis_index("rhs")
    core = mine + 1 - 2 * lax.rem(mine, 2)
    across = lax.rem(mine + 2, 4)

    lvl_in[...] = jnp.zeros_like(lvl_in)
    barrier = pltpu.get_barrier_semaphore()
    for other in (core, across):
        pl.semaphore_signal(barrier, inc=1, device_id=(me, other), device_id_type=MESH)
    for d in range(1, REACH):
        @pl.when(me + d < n)
        def _():
            pl.semaphore_signal(barrier, inc=1, device_id=(me + d, mine), device_id_type=MESH)

        @pl.when(me >= d)
        def _():
            pl.semaphore_signal(barrier, inc=1, device_id=(me - d, mine), device_id_type=MESH)

    own = [level_ref[r] for r in range(rows)]

    def ranked(levels, base):
        out = []
        for r in range(rows):
            before = jnp.int32(0)
            for q in range(rows):
                if q < r:
                    before += (levels[q] <= levels[r]).astype(jnp.int32)
                elif q > r:
                    before += (levels[q] < levels[r]).astype(jnp.int32)
            rank[base + r] = before
            out.append(before)
        return out

    own_rank = ranked(own, BELOW * rows)
    where = []
    for p in range(rows):
        at = jnp.int32(0)
        for r in range(rows):
            at += jnp.where(own_rank[r] == p, r, 0)
        perm[p] = at
        lev[p] = level_ref[at]
        where.append(at)

    def span(who):
        return pl.ds(pl.multiple_of(who * part, part), part)

    def stage_diag(p):
        inv[p, span(mine), :] = diag_ref[where[p]]

    def stage_off(p):
        for k in range(kk):
            fac[p - 1, span(mine), k * bs:(k + 1) * bs] = off_ref[where[p], k]

    half = rows // 2
    items = [("d", 0)] + [("o", p) for p in range(1, half)] + [("d", 1)] + [("o", p) for p in range(half, rows)]

    def piece(item, who):
        kind, at = item
        if kind == "d":
            return inv.at[at * half:(at + 1) * half, span(who), :]
        return fac.at[at - 1, span(who), :]

    def send_x(i):
        return pltpu.make_async_remote_copy(
            piece(items[i], mine), piece(items[i], mine), x_send.at[i], x_recv.at[i],
            device_id=(me, across), device_id_type=MESH)

    def send_c(i):
        return pltpu.make_async_remote_copy(
            piece(items[i], mine), piece(items[i], mine), c_send.at[i], c_recv.at[i],
            device_id=(me, core), device_id_type=MESH)

    def send_f(i):
        return pltpu.make_async_remote_copy(
            piece(items[i], across), piece(items[i], across), f_send.at[i], f_recv.at[i],
            device_id=(me, core), device_id_type=MESH)

    def issue(i):
        if i < len(items):
            send_x(i).start()
            send_c(i).start()

    def arrive(i):
        send_x(i).wait_recv()
        send_f(i).start()
        send_x(i).wait_send()
        issue(i + AHEAD)
        send_c(i).wait_recv()
        send_f(i).wait_recv()

    for p in range(rows):
        stage_diag(p)
        if p > 0:
            stage_off(p)

    greeted = jnp.int32(2)
    for d in range(1, REACH):
        greeted += (me + d < n).astype(jnp.int32) + (me >= d).astype(jnp.int32)
    pl.semaphore_wait(barrier, greeted)

    for i in range(AHEAD):
        issue(i)

    def upward(src, dst, s, r, d):
        return pltpu.make_async_remote_copy(
            src, dst, s, r, device_id=(me + d, mine), device_id_type=MESH)

    def send_lvl(d):
        return upward(lvl_ref, lvl_in.at[BELOW - d], lvl_send.at[d - 1], lvl_recv.at[d - 1], d)

    def send_0(d):
        return upward(sol0, land0.at[BELOW - d], w0_send.at[d - 1], w0_recv.at[d - 1], d)

    def send_1(i, d):
        return upward(sol1.at[i], land1.at[BELOW - d, i], w1_send.at[i, d - 1], w1_recv.at[i, d - 1], d)

    def send_2(i, d):
        return upward(sol2.at[i], land2.at[BELOW - d, i], w2_send.at[i, d - 1], w2_recv.at[i, d - 1], d)

    def each_up(what):
        for d in range(1, REACH):
            @pl.when(me + d < n)
            def _():
                what(d)

    def each_down(what):
        for d in range(1, REACH):
            @pl.when(me >= d)
            def _():
                what(d)

    each_up(lambda d: send_lvl(d).start())

    arrive(0)
    for p in range(half):
        sol0[p] = nt(right_ref[where[p]], inv[p]).astype(jnp.bfloat16)
    each_up(lambda d: send_0(d).start())

    each_down(lambda d: send_lvl(d).wait_recv())
    fetch = pltpu.make_async_copy(lvl_in, lvl_s, lvl_sem)
    fetch.start()
    fetch.wait()
    for o in range(BELOW):
        ranked([lvl_s[o, r, 0] for r in range(rows)], o * rows)

    def picked(p):
        taken = []
        for k in range(kk):
            at = cols_ref[perm[p], k] - (me - BELOW) * rows
            at = jnp.clip(at, 0, REACH * rows - 1)
            taken.append(win[at - lax.rem(at, rows) + rank[at]])
        return jnp.concatenate(taken, axis=1)

    def solve(p):
        contribution = nt(picked(p), fac[p - 1])
        residue = (right_ref[perm[p]].astype(jnp.float32) - contribution).astype(jnp.bfloat16)
        return nt(residue, inv[p])

    def keep(p, level_now, updated, before):
        if before is None:
            return updated.astype(jnp.bfloat16)
        return jnp.where(lev[p] == level_now, updated, before.astype(jnp.float32)).astype(jnp.bfloat16)

    def fill(land, sol, first):
        count = sol.shape[0]
        for d in range(1, REACH):
            o = BELOW - d
            win[o * rows + first:o * rows + first + count] = land[o]
        win[BELOW * rows + first:BELOW * rows + first + count] = sol[...]

    each_down(lambda d: send_0(d).wait_recv())
    fill(land0, sol0, 0)

    at_item = {p: items.index(("o", p)) for p in range(1, rows)}
    for p in range(FIRST[1], LAST[1] + 1):
        if p == half:
            arrive(half)
        arrive(at_item[p])
        i = p - FIRST[1]
        sol1[i] = keep(p, 1, solve(p), sol0[p] if p <= LAST[0] else None)
        each_up(lambda d: send_1(i, d).start())
    count1 = LAST[1] - FIRST[1] + 1
    each_down(lambda d: [send_1(i, d).wait_recv() for i in range(count1)])
    fill(land1, sol1, FIRST[1])

    for p in range(FIRST[2], LAST[2] + 1):
        if p == LAST[2]:
            arrive(at_item[p])
        i = p - FIRST[2]
        sol2[i] = keep(p, 2, solve(p), sol1[p - FIRST[1]] if p <= LAST[1] else None)
        each_up(lambda d: send_2(i, d).start())
    count2 = LAST[2] - FIRST[2] + 1
    arrive(at_item[rows - 1])
    each_down(lambda d: [send_2(i, d).wait_recv() for i in range(count2)])
    fill(land2, sol2, FIRST[2])

    fin[0] = sol0[0]
    fin[1] = sol1[0]
    for p in range(FIRST[2], FIRST[3]):
        fin[p] = sol2[p - FIRST[2]]
    for p in range(FIRST[3], rows):
        fin[p] = keep(p, 3, solve(p), sol2[p - FIRST[2]] if p <= LAST[2] else None)
    for r in range(rows):
        out_ref[r] = fin[rank[BELOW * rows + r]]

    for i in range(len(items)):
        send_c(i).wait_send()
        send_f(i).wait_send()

    def drain(d):
        send_lvl(d).wait_send()
        send_0(d).wait_send()
        for i in range(count1):
            send_1(i, d).wait_send()
        for i in range(count2):
            send_2(i, d).wait_send()

    each_up(drain)


def per_device(n, right_side, off_blocks, diag_inverse, block_level, block_columns):
    rows, kk, part, bs = off_blocks.shape
    samples = right_side.shape[1]
    vmem = pl.BlockSpec(memory_space=pltpu.VMEM)
    smem = pl.BlockSpec(memory_space=pltpu.SMEM)
    tile = (samples, bs)
    counts = [b - a + 1 for a, b in zip(FIRST, LAST)]
    items = rows + 1
    dma = pltpu.SemaphoreType.DMA
    return pl.pallas_call(
        functools.partial(kernel, n),
        out_shape=jax.ShapeDtypeStruct(right_side.shape, jnp.bfloat16),
        in_specs=[smem, smem, vmem, vmem, vmem, vmem],
        out_specs=vmem,
        scratch_shapes=[
            pltpu.VMEM((rows - 1, 4 * part, kk * bs), jnp.bfloat16),
            pltpu.VMEM((rows, 4 * part, bs), jnp.bfloat16),
            pltpu.VMEM((REACH * rows,) + tile, jnp.bfloat16),
            pltpu.VMEM((BELOW, counts[0]) + tile, jnp.bfloat16),
            pltpu.VMEM((BELOW, counts[1]) + tile, jnp.bfloat16),
            pltpu.VMEM((BELOW, counts[2]) + tile, jnp.bfloat16),
            pltpu.VMEM((counts[0],) + tile, jnp.bfloat16),
            pltpu.VMEM((counts[1],) + tile, jnp.bfloat16),
            pltpu.VMEM((counts[2],) + tile, jnp.bfloat16),
            pltpu.VMEM((rows,) + tile, jnp.bfloat16),
            pltpu.VMEM((BELOW, rows, 128), jnp.int32),
            pltpu.SMEM((BELOW, rows, 128), jnp.int32),
            pltpu.SMEM((REACH * rows,), jnp.int32),
            pltpu.SMEM((rows,), jnp.int32),
            pltpu.SMEM((rows,), jnp.int32),
            dma((BELOW,)), dma((BELOW,)), dma,
            dma((items,)), dma((items,)), dma((items,)), dma((items,)), dma((items,)), dma((items,)),
            dma((BELOW,)), dma((BELOW,)),
            dma((counts[1], BELOW)), dma((counts[1], BELOW)),
            dma((counts[2], BELOW)), dma((counts[2], BELOW)),
        ],
        compiler_params=pltpu.CompilerParams(
            collective_id=0, has_side_effects=True, vmem_limit_bytes=48 * 2 ** 20),
    )(
        block_level, block_columns,
        jnp.broadcast_to(block_level[:, None], (rows, 128)),
        right_side, off_blocks, diag_inverse,
    )


def solution(mesh):
    return jax.shard_map(
        functools.partial(per_device, mesh.shape["rows"]),
        mesh=mesh,
        in_specs=(
            P("rows", "rhs", None),
            P("rows", None, "rhs", None),
            P("rows", "rhs", None),
            P("rows"),
            P("rows", None),
        ),
        out_specs=P("rows", "rhs", None),
        check_vma=False,
    )
```

time: 225 us -> 102 us (0.45)
  the two profiles are of different devices: /device:TPU:16 before, /device:TPU:25 now
where the time goes in v1:
time: 102 us; the launch traced here: 101 us
  Pallas kernels  95 us (93%)
  local copies, waits for them, and re-layouts  6.44 us (6%)
    pallas_call x1, Pallas kernels, per_device(): pl.pallas_call(functools.partial(kernel, n), out_shape=jax.ShapeDtypeStru...  95 us
    unnamed x11, local copies, waits for them, and re-layouts  5.72 us

profile of v1, /device:TPU:25, one launch (start us, length us, event | category | flops | bytes accessed | tf_op | source)
XLA Modules:
  0.0 101.4 jit_solution(4510295858719421765)
XLA Ops:
  0.0 0.7 broadcast_in_dim.2.lvl_ref
  0.7 0.0 copy-start
  0.7 1.6 %copy-done = bf16[8,8,64,256]{3,2,1,0:T(8,128)(2,1)S(1)} copy-done((bf16[8,8,64,256]{3,2,1,0:T(8,128)(2,1)S(1)}, bf16[8,8,64,256]{3,2,1,0:T(8,128)(2,1)}, u32[]{:S(2)}) %copy-start) | copy-done | bytes 2097176
  2.3 0.0 copy-start.1
  2.3 1.0 %copy-done.1 = bf16[8,128,256]{2,1,0:T(8,128)(2,1)S(1)} copy-done((bf16[8,128,256]{2,1,0:T(8,128)(2,1)S(1)}, bf16[8,128,256]{2,1,0:T(8,128)(2,1)}, u32[]{:S(2)}) %copy-start.1) | copy-done | bytes 524312
  3.4 0.0 copy-start.2
  3.4 0.9 copy-done.2
  4.3 0.0 copy-start.3
  4.3 0.7 copy-done.3
  5.0 0.0 copy-start.4
  5.0 0.7 copy-done.4
  5.7 95.0 %shard_map.55 = bf16[8,128,256]{2,1,0:T(8,128)(2,1)S(1)} custom-call(s32[8]{0:T(128)S(1)} %copy-done.4, s32[8,8]{1,0:T(8,128)S(1)} %copy-done.3, s32[8,128]{1,0:T(8,128)S(1)} %broadcast_in_dim.2.lvl_ref, bf16[8,128,256]{2,1,0:T(8,128)(2,1)S(1)} %copy-done.1, bf16[8,8,64,256]{3,2,1,0:T(8,128)(2,1)S(1)} %copy-done, bf16[8,64,256]{2,1,0:T(8,128)(2,1)S(1)} %copy-done.2), custom_call_target="tpu_custom_call" | custom-call | tf_op jit(solution)/shard_map/pallas_call | solution.py:257
  100.6 0.8 copy.7
Async XLA Ops:
  0.7 1.6 %copy-start = (bf16[8,8,64,256]{3,2,1,0:T(8,128)(2,1)S(1)}, bf16[8,8,64,256]{3,2,1,0:T(8,128)(2,1)}, u32[]{:S(2)}) copy-start(bf16[8,8,64,256]{3,2,1,0:T(8,128)(2,1)} %off_ref.1) | copy-start | bytes 6291460
  2.3 1.0 %copy-start.1 = (bf16[8,128,256]{2,1,0:T(8,128)(2,1)S(1)}, bf16[8,128,256]{2,1,0:T(8,128)(2,1)}, u32[]{:S(2)}) copy-start(bf16[8,128,256]{2,1,0:T(8,128)(2,1)} %right_ref.1) | copy-start | bytes 1572868
  3.4 0.9 copy-start.2
  4.3 0.7 copy-start.3
  5.0 0.7 copy-start.4

commit v2 on v1

--- a/solution.py
+++ b/solution.py
@@ -128,21 +128,10 @@
     for i in range(AHEAD):
         issue(i)
 
-    def upward(src, dst, s, r, d):
-        return pltpu.make_async_remote_copy(
-            src, dst, s, r, device_id=(me + d, mine), device_id_type=MESH)
-
     def send_lvl(d):
-        return upward(lvl_ref, lvl_in.at[BELOW - d], lvl_send.at[d - 1], lvl_recv.at[d - 1], d)
-
-    def send_0(d):
-        return upward(sol0, land0.at[BELOW - d], w0_send.at[d - 1], w0_recv.at[d - 1], d)
-
-    def send_1(i, d):
-        return upward(sol1.at[i], land1.at[BELOW - d, i], w1_send.at[i, d - 1], w1_recv.at[i, d - 1], d)
-
-    def send_2(i, d):
-        return upward(sol2.at[i], land2.at[BELOW - d, i], w2_send.at[i, d - 1], w2_recv.at[i, d - 1], d)
+        return pltpu.make_async_remote_copy(
+            lvl_ref, lvl_in.at[BELOW - d], lvl_send.at[d - 1], lvl_recv.at[d - 1],
+            device_id=(me + d, mine), device_id_type=MESH)
 
     def each_up(what):
         for d in range(1, REACH):
@@ -156,12 +145,86 @@
             def _():
                 what(d)
 
+    even = lax.rem(me, 2) == 0
+    odd = lax.rem(me, 2) == 1
+    sols, lands = (sol0, sol1, sol2), (land0, land1, land2)
+    hop_send, hop_recv = (w0_send, w1_send, w2_send), (w0_recv, w1_recv, w2_recv)
+    OWN_UP, OWN_SIDE, PASS_SIDE, PASS_UP = range(4)
+
+    def hop(v, i, way, to, d):
+        src = sols[v].at[i]
+        if way == PASS_SIDE:
+            src = lands[v].at[BELOW - 2, i]
+        if way == PASS_UP:
+            src = lands[v].at[BELOW - 1, i]
+        return pltpu.make_async_remote_copy(
+            src, lands[v].at[BELOW - d, i], hop_send[v].at[i, way], hop_recv[v].at[i, d - 1],
+            device_id=(to, mine), device_id_type=MESH)
+
+    def landed(v, i, d):
+        hop(v, i, OWN_UP, me, d).wait_recv()
+
+    def own_hops(v, i, what):
+        @pl.when(me + 2 < n)
+        def _():
+            what(hop(v, i, OWN_UP, me + 2, 2))
+
+        @pl.when(even)
+        def _():
+            what(hop(v, i, OWN_SIDE, me + 1, 1))
+
+    def side_hops(v, i, what):
+        @pl.when(even & (me >= 2))
+        def _():
+            what(hop(v, i, PASS_SIDE, me + 1, 3))
+
+        @pl.when(odd & (me >= 2))
+        def _():
+            what(hop(v, i, PASS_SIDE, me - 1, 1))
+
+    def up_hops(v, i, what):
+        @pl.when(even & (me >= 2) & (me + 2 < n))
+        def _():
+            what(hop(v, i, PASS_UP, me + 2, 3))
+
+    def start(copy):
+        copy.start()
+
+    def first_leg(v, i):
+        @pl.when(me >= 2)
+        def _():
+            landed(v, i, 2)
+        side_hops(v, i, start)
+
+    def second_leg(v, i):
+        @pl.when(me >= 1)
+        def _():
+            landed(v, i, 1)
+        up_hops(v, i, start)
+
+    def third_leg(v, i):
+        @pl.when(me >= 3)
+        def _():
+            landed(v, i, 3)
+
+    def serve(v, i):
+        count = sols[v].shape[0]
+        for leg, late in ((first_leg, 1), (second_leg, 2), (third_leg, 3)):
+            if 0 <= i - late < count:
+                leg(v, i - late)
+
+    def serve_rest(v):
+        count = sols[v].shape[0]
+        for i in range(count, count + 3):
+            serve(v, i)
+
     each_up(lambda d: send_lvl(d).start())
 
+    at_item = {p: items.index(("o", p)) for p in range(1, rows)}
     arrive(0)
     for p in range(half):
         sol0[p] = nt(right_ref[where[p]], inv[p]).astype(jnp.bfloat16)
-    each_up(lambda d: send_0(d).start())
+        own_hops(0, p, start)
 
     each_down(lambda d: send_lvl(d).wait_recv())
     fetch = pltpu.make_async_copy(lvl_in, lvl_s, lvl_sem)
@@ -195,19 +258,23 @@
             win[o * rows + first:o * rows + first + count] = land[o]
         win[BELOW * rows + first:BELOW * rows + first + count] = sol[...]
 
-    each_down(lambda d: send_0(d).wait_recv())
+    arrive(at_item[1])
+    for i in range(half):
+        serve(0, i)
+    arrive(at_item[2])
+    serve_rest(0)
     fill(land0, sol0, 0)
 
-    at_item = {p: items.index(("o", p)) for p in range(1, rows)}
     for p in range(FIRST[1], LAST[1] + 1):
         if p == half:
             arrive(half)
-        arrive(at_item[p])
+        if p > 2:
+            arrive(at_item[p])
         i = p - FIRST[1]
         sol1[i] = keep(p, 1, solve(p), sol0[p] if p <= LAST[0] else None)
-        each_up(lambda d: send_1(i, d).start())
-    count1 = LAST[1] - FIRST[1] + 1
-    each_down(lambda d: [send_1(i, d).wait_recv() for i in range(count1)])
+        own_hops(1, i, start)
+        serve(1, i)
+    serve_rest(1)
     fill(land1, sol1, FIRST[1])
 
     for p in range(FIRST[2], LAST[2] + 1):
@@ -215,10 +282,10 @@
             arrive(at_item[p])
         i = p - FIRST[2]
         sol2[i] = keep(p, 2, solve(p), sol1[p - FIRST[1]] if p <= LAST[1] else None)
-        each_up(lambda d: send_2(i, d).start())
-    count2 = LAST[2] - FIRST[2] + 1
+        own_hops(2, i, start)
+        serve(2, i)
     arrive(at_item[rows - 1])
-    each_down(lambda d: [send_2(i, d).wait_recv() for i in range(count2)])
+    serve_rest(2)
     fill(land2, sol2, FIRST[2])
 
     fin[0] = sol0[0]
@@ -234,15 +301,11 @@
         send_c(i).wait_send()
         send_f(i).wait_send()
 
-    def drain(d):
-        send_lvl(d).wait_send()
-        send_0(d).wait_send()
-        for i in range(count1):
-            send_1(i, d).wait_send()
-        for i in range(count2):
-            send_2(i, d).wait_send()
-
-    each_up(drain)
+    each_up(lambda d: send_lvl(d).wait_send())
+    for v in range(BELOW):
+        for i in range(sols[v].shape[0]):
+            for hops in (own_hops, side_hops, up_hops):
+                hops(v, i, lambda copy: copy.wait_send())
 
 
 def per_device(n, right_side, off_blocks, diag_inverse, block_level, block_columns):
@@ -277,9 +340,9 @@
             pltpu.SMEM((rows,), jnp.int32),
             dma((BELOW,)), dma((BELOW,)), dma,
             dma((items,)), dma((items,)), dma((items,)), dma((items,)), dma((items,)), dma((items,)),
-            dma((BELOW,)), dma((BELOW,)),
-            dma((counts[1], BELOW)), dma((counts[1], BELOW)),
-            dma((counts[2], BELOW)), dma((counts[2], BELOW)),
+            dma((counts[0], 4)), dma((counts[0], BELOW)),
+            dma((counts[1], 4)), dma((counts[1], BELOW)),
+            dma((counts[2], 4)), dma((counts[2], BELOW)),
         ],
         compiler_params=pltpu.CompilerParams(
             collective_id=0, has_side_effects=True, vmem_limit_bytes=48 * 2 ** 20),

time: 102 us -> 79.6 us (0.78)
  Pallas kernels: 95 us -> 72.7 us
    pallas_call x1, Pallas kernels: 95 us -> 72.7 us  [per_device(): pl.pallas_call(functools.partial(kernel, n), out_shape=jax.ShapeDtypeStru...]
where the time goes in v2:
time: 79.6 us; the launch traced here: 79.1 us
  Pallas kernels  72.7 us (91%)
  local copies, waits for them, and re-layouts  6.44 us (8%)
    pallas_call x1, Pallas kernels, per_device(): pl.pallas_call(functools.partial(kernel, n), out_shape=jax.ShapeDtypeStru...  72.7 us
    unnamed x11, local copies, waits for them, and re-layouts  5.72 us

profile of v2, /device:TPU:25, one launch (start us, length us, event | category | flops | bytes accessed | tf_op | source)
XLA Modules:
  0.0 79.1 jit_solution(6160638306760756465)
XLA Ops:
  0.0 0.7 broadcast_in_dim.2.lvl_ref
  0.7 0.0 copy-start
  0.7 1.6 %copy-done = bf16[8,8,64,256]{3,2,1,0:T(8,128)(2,1)S(1)} copy-done((bf16[8,8,64,256]{3,2,1,0:T(8,128)(2,1)S(1)}, bf16[8,8,64,256]{3,2,1,0:T(8,128)(2,1)}, u32[]{:S(2)}) %copy-start) | copy-done | bytes 2097176
  2.3 0.0 copy-start.1
  2.3 1.0 %copy-done.1 = bf16[8,128,256]{2,1,0:T(8,128)(2,1)S(1)} copy-done((bf16[8,128,256]{2,1,0:T(8,128)(2,1)S(1)}, bf16[8,128,256]{2,1,0:T(8,128)(2,1)}, u32[]{:S(2)}) %copy-start.1) | copy-done | bytes 524312
  3.4 0.0 copy-start.2
  3.4 0.9 %copy-done.2 = bf16[8,64,256]{2,1,0:T(8,128)(2,1)S(1)} copy-done((bf16[8,64,256]{2,1,0:T(8,128)(2,1)S(1)}, bf16[8,64,256]{2,1,0:T(8,128)(2,1)}, u32[]{:S(2)}) %copy-start.2) | copy-done | bytes 262168
  4.3 0.0 copy-start.3
  4.3 0.7 copy-done.3
  5.0 0.0 copy-start.4
  5.0 0.7 copy-done.4
  5.7 72.7 %shard_map.55 = bf16[8,128,256]{2,1,0:T(8,128)(2,1)S(1)} custom-call(s32[8]{0:T(128)S(1)} %copy-done.4, s32[8,8]{1,0:T(8,128)S(1)} %copy-done.3, s32[8,128]{1,0:T(8,128)S(1)} %broadcast_in_dim.2.lvl_ref, bf16[8,128,256]{2,1,0:T(8,128)(2,1)S(1)} %copy-done.1, bf16[8,8,64,256]{3,2,1,0:T(8,128)(2,1)S(1)} %copy-done, bf16[8,64,256]{2,1,0:T(8,128)(2,1)S(1)} %copy-done.2), custom_call_target="tpu_custom_call" | custom-call | tf_op jit(solution)/shard_map/pallas_call | solution.py:320
  78.3 0.8 %copy.7 = bf16[8,128,256]{2,1,0:T(8,128)(2,1)} copy(bf16[8,128,256]{2,1,0:T(8,128)(2,1)S(1)} %shard_map.55) | data formatting | bytes 1048576
Async XLA Ops:
  0.7 1.6 %copy-start = (bf16[8,8,64,256]{3,2,1,0:T(8,128)(2,1)S(1)}, bf16[8,8,64,256]{3,2,1,0:T(8,128)(2,1)}, u32[]{:S(2)}) copy-start(bf16[8,8,64,256]{3,2,1,0:T(8,128)(2,1)} %off_ref.1) | copy-start | bytes 6291460
  2.3 1.0 %copy-start.1 = (bf16[8,128,256]{2,1,0:T(8,128)(2,1)S(1)}, bf16[8,128,256]{2,1,0:T(8,128)(2,1)}, u32[]{:S(2)}) copy-start(bf16[8,128,256]{2,1,0:T(8,128)(2,1)} %right_ref.1) | copy-start | bytes 1572868
  3.4 0.9 %copy-start.2 = (bf16[8,64,256]{2,1,0:T(8,128)(2,1)S(1)}, bf16[8,64,256]{2,1,0:T(8,128)(2,1)}, u32[]{:S(2)}) copy-start(bf16[8,64,256]{2,1,0:T(8,128)(2,1)} %diag_ref.1) | copy-start | bytes 786436
  4.3 0.7 copy-start.3
  5.0 0.7 copy-start.4

commit v3 on v2

--- a/solution.py
+++ b/solution.py
@@ -12,6 +12,9 @@
 MESH = pl.DeviceIdType.MESH
 FIRST = (0, 1, 2, 4)
 LAST = (3, 5, 6, 7)
+COUNTS = (4, 5, 4)
+BASE = (0, 4, 9, 13)
+HELD = 13
 AHEAD = 3
 
 
@@ -20,8 +23,8 @@
 
 
 def kernel(
-    n, level_ref, cols_ref, lvl_ref, right_ref, off_ref, diag_ref, out_ref,
-    fac, inv, win, land0, land1, land2, sol0, sol1, sol2, fin, lvl_in, lvl_s, rank, perm, lev,
+    n, level_ref, cols_ref, right_ref, off_ref, diag_ref, out_ref,
+    fac, fac_last, inv, win, land0, land1, land2, sol0, sol1, sol2, lvl_ref, lvl_in, lvl_s, slot, perm,
     lvl_send, lvl_recv, lvl_sem, x_send, x_recv, c_send, c_recv, f_send, f_recv,
     w0_send, w0_recv, w1_send, w1_recv, w2_send, w2_recv,
 ):
@@ -31,6 +34,8 @@
     across = lax.rem(mine + 2, 4)
 
     lvl_in[...] = jnp.zeros_like(lvl_in)
+    for r in range(rows):
+        lvl_ref[r:r + 1, :] = jnp.full((1, lvl_ref.shape[1]), level_ref[r], jnp.int32)
     barrier = pltpu.get_barrier_semaphore()
     for other in (core, across):
         pl.semaphore_signal(barrier, inc=1, device_id=(me, other), device_id_type=MESH)
@@ -47,6 +52,9 @@
 
     def ranked(levels, base):
         out = []
+        lower = jnp.int32(0)
+        for r in range(rows):
+            lower += (levels[r] < 2).astype(jnp.int32)
         for r in range(rows):
             before = jnp.int32(0)
             for q in range(rows):
@@ -54,18 +62,20 @@
                     before += (levels[q] <= levels[r]).astype(jnp.int32)
                 elif q > r:
                     before += (levels[q] < levels[r]).astype(jnp.int32)
-            rank[base + r] = before
+            at = jnp.where(levels[r] == 0, before, before - FIRST[1] + BASE[1])
+            at = jnp.where(levels[r] == 2, before - lower + BASE[2], at)
+            at = jnp.where(levels[r] == 3, before - FIRST[3] + BASE[3], at)
+            slot[base * rows + r] = jnp.clip(at + base * HELD, 0, win.shape[0] - 1)
             out.append(before)
-        return out
-
-    own_rank = ranked(own, BELOW * rows)
+        return out, lower
+
+    own_rank, lower2 = ranked(own, BELOW)
     where = []
     for p in range(rows):
         at = jnp.int32(0)
         for r in range(rows):
             at += jnp.where(own_rank[r] == p, r, 0)
         perm[p] = at
-        lev[p] = level_ref[at]
         where.append(at)
 
     def span(who):
@@ -76,15 +86,22 @@
 
     def stage_off(p):
         for k in range(kk):
-            fac[p - 1, span(mine), k * bs:(k + 1) * bs] = off_ref[where[p], k]
+            if p == rows - 1:
+                fac_last[span(mine), k * bs:(k + 1) * bs] = off_ref[where[p], k]
+            else:
+                fac[p - 1, span(mine), k * bs:(k + 1) * bs] = off_ref[where[p], k]
 
     half = rows // 2
-    items = [("d", 0)] + [("o", p) for p in range(1, half)] + [("d", 1)] + [("o", p) for p in range(half, rows)]
+    early = LAST[1] + 1
+    items = [("d", (0, half))] + [("o", p) for p in range(1, half)] + [("d", (half, early))]
+    items += [("o", p) for p in range(half, early)] + [("d", (early, rows))] + [("o", p) for p in range(early, rows)]
 
     def piece(item, who):
         kind, at = item
         if kind == "d":
-            return inv.at[at * half:(at + 1) * half, span(who), :]
+            return inv.at[at[0]:at[1], span(who), :]
+        if at == rows - 1:
+            return fac_last.at[span(who), :]
         return fac.at[at - 1, span(who), :]
 
     def send_x(i):
@@ -231,71 +248,61 @@
     fetch.start()
     fetch.wait()
     for o in range(BELOW):
-        ranked([lvl_s[o, r, 0] for r in range(rows)], o * rows)
-
-    def picked(p):
+        ranked([lvl_s[o, r, 0] for r in range(rows)], o)
+
+    def solve(p, factor, inverse):
+        row = perm[p]
         taken = []
         for k in range(kk):
-            at = cols_ref[perm[p], k] - (me - BELOW) * rows
-            at = jnp.clip(at, 0, REACH * rows - 1)
-            taken.append(win[at - lax.rem(at, rows) + rank[at]])
-        return jnp.concatenate(taken, axis=1)
-
-    def solve(p):
-        contribution = nt(picked(p), fac[p - 1])
-        residue = (right_ref[perm[p]].astype(jnp.float32) - contribution).astype(jnp.bfloat16)
-        return nt(residue, inv[p])
-
-    def keep(p, level_now, updated, before):
-        if before is None:
-            return updated.astype(jnp.bfloat16)
-        return jnp.where(lev[p] == level_now, updated, before.astype(jnp.float32)).astype(jnp.bfloat16)
-
-    def fill(land, sol, first):
-        count = sol.shape[0]
+            at = cols_ref[row, k] - (me - BELOW) * rows
+            taken.append(win[slot[jnp.clip(at, 0, REACH * rows - 1)]])
+        contribution = nt(jnp.concatenate(taken, axis=1), factor)
+        residue = (right_ref[row].astype(jnp.float32) - contribution).astype(jnp.bfloat16)
+        return nt(residue, inverse).astype(jnp.bfloat16)
+
+    def fill(v):
         for d in range(1, REACH):
-            o = BELOW - d
-            win[o * rows + first:o * rows + first + count] = land[o]
-        win[BELOW * rows + first:BELOW * rows + first + count] = sol[...]
+            o = (BELOW - d) * HELD + BASE[v]
+            win[o:o + COUNTS[v]] = lands[v][BELOW - d]
+        o = BELOW * HELD + BASE[v]
+        win[o:o + COUNTS[v]] = sols[v][...]
 
     arrive(at_item[1])
     for i in range(half):
         serve(0, i)
     arrive(at_item[2])
     serve_rest(0)
-    fill(land0, sol0, 0)
+    fill(0)
 
     for p in range(FIRST[1], LAST[1] + 1):
         if p == half:
-            arrive(half)
+            arrive(items.index(("d", (half, early))))
         if p > 2:
             arrive(at_item[p])
         i = p - FIRST[1]
-        sol1[i] = keep(p, 1, solve(p), sol0[p] if p <= LAST[0] else None)
+        sol1[i] = solve(p, fac[p - 1], inv[p])
         own_hops(1, i, start)
         serve(1, i)
     serve_rest(1)
-    fill(land1, sol1, FIRST[1])
-
-    for p in range(FIRST[2], LAST[2] + 1):
-        if p == LAST[2]:
-            arrive(at_item[p])
-        i = p - FIRST[2]
-        sol2[i] = keep(p, 2, solve(p), sol1[p - FIRST[1]] if p <= LAST[1] else None)
+    fill(1)
+
+    arrive(items.index(("d", (early, rows))))
+    for p in range(early, rows - 1):
+        arrive(at_item[p])
+    for i in range(COUNTS[2]):
+        p = jnp.clip(lower2 + i, FIRST[2], LAST[2])
+        sol2[i] = solve(p, fac[p - 1], inv[p])
         own_hops(2, i, start)
         serve(2, i)
     arrive(at_item[rows - 1])
     serve_rest(2)
-    fill(land2, sol2, FIRST[2])
-
-    fin[0] = sol0[0]
-    fin[1] = sol1[0]
-    for p in range(FIRST[2], FIRST[3]):
-        fin[p] = sol2[p - FIRST[2]]
+    fill(2)
+
+    o = BELOW * HELD + BASE[3] - FIRST[3]
     for p in range(FIRST[3], rows):
-        fin[p] = keep(p, 3, solve(p), sol2[p - FIRST[2]] if p <= LAST[2] else None)
+        win[o + p] = solve(p, fac_last[...] if p == rows - 1 else fac[p - 1], inv[p])
     for r in range(rows):
-        out_ref[r] = fin[rank[BELOW * rows + r]]
+        out_ref[r] = win[slot[BELOW * rows + r]]
 
     for i in range(len(items)):
         send_c(i).wait_send()
@@ -314,29 +321,29 @@
     vmem = pl.BlockSpec(memory_space=pltpu.VMEM)
     smem = pl.BlockSpec(memory_space=pltpu.SMEM)
     tile = (samples, bs)
-    counts = [b - a + 1 for a, b in zip(FIRST, LAST)]
-    items = rows + 1
+    counts = COUNTS
+    items = rows + 2
     dma = pltpu.SemaphoreType.DMA
     return pl.pallas_call(
         functools.partial(kernel, n),
         out_shape=jax.ShapeDtypeStruct(right_side.shape, jnp.bfloat16),
-        in_specs=[smem, smem, vmem, vmem, vmem, vmem],
+        in_specs=[smem, smem, vmem, vmem, vmem],
         out_specs=vmem,
         scratch_shapes=[
-            pltpu.VMEM((rows - 1, 4 * part, kk * bs), jnp.bfloat16),
+            pltpu.VMEM((rows - 2, 4 * part, kk * bs), jnp.bfloat16),
+            pltpu.VMEM((4 * part, kk * bs), jnp.bfloat16),
             pltpu.VMEM((rows, 4 * part, bs), jnp.bfloat16),
-            pltpu.VMEM((REACH * rows,) + tile, jnp.bfloat16),
+            pltpu.VMEM((REACH * HELD + rows - FIRST[3],) + tile, jnp.bfloat16),
             pltpu.VMEM((BELOW, counts[0]) + tile, jnp.bfloat16),
             pltpu.VMEM((BELOW, counts[1]) + tile, jnp.bfloat16),
             pltpu.VMEM((BELOW, counts[2]) + tile, jnp.bfloat16),
             pltpu.VMEM((counts[0],) + tile, jnp.bfloat16),
             pltpu.VMEM((counts[1],) + tile, jnp.bfloat16),
             pltpu.VMEM((counts[2],) + tile, jnp.bfloat16),
-            pltpu.VMEM((rows,) + tile, jnp.bfloat16),
+            pltpu.VMEM((rows, 128), jnp.int32),
             pltpu.VMEM((BELOW, rows, 128), jnp.int32),
             pltpu.SMEM((BELOW, rows, 128), jnp.int32),
             pltpu.SMEM((REACH * rows,), jnp.int32),
-            pltpu.SMEM((rows,), jnp.int32),
             pltpu.SMEM((rows,), jnp.int32),
             dma((BELOW,)), dma((BELOW,)), dma,
             dma((items,)), dma((items,)), dma((items,)), dma((items,)), dma((items,)), dma((items,)),
@@ -347,9 +354,7 @@
         compiler_params=pltpu.CompilerParams(
             collective_id=0, has_side_effects=True, vmem_limit_bytes=48 * 2 ** 20),
     )(
-        block_level, block_columns,
-        jnp.broadcast_to(block_level[:, None], (rows, 128)),
-        right_side, off_blocks, diag_inverse,
+        block_level, block_columns, right_side, off_blocks, diag_inverse,
     )
 
 

time: 79.6 us -> 76.8 us (0.965)
  Pallas kernels: 72.7 us -> 70.8 us
    pallas_call x1, Pallas kernels: 72.7 us -> 70.8 us  [per_device(): pl.pallas_call(functools.partial(kernel, n), out_shape=jax.ShapeDtypeStru...]
where the time goes in v3:
time: 76.8 us; the launch traced here: 76.5 us
  Pallas kernels  70.8 us (92%)
  local copies, waits for them, and re-layouts  5.72 us (7%)
    pallas_call x1, Pallas kernels, per_device(): pl.pallas_call(functools.partial(kernel, n), out_shape=jax.ShapeDtypeStru...  70.8 us
    unnamed x11, local copies, waits for them, and re-layouts  5.72 us

profile of v3, /device:TPU:25, one launch (start us, length us, event | category | flops | bytes accessed | tf_op | source)
XLA Modules:
  0.0 76.5 jit_solution(3754735115120510940)
XLA Ops:
  0.0 0.0 copy-start
  0.0 1.6 %copy-done = bf16[8,8,64,256]{3,2,1,0:T(8,128)(2,1)S(1)} copy-done((bf16[8,8,64,256]{3,2,1,0:T(8,128)(2,1)S(1)}, bf16[8,8,64,256]{3,2,1,0:T(8,128)(2,1)}, u32[]{:S(2)}) %copy-start) | copy-done | bytes 2097176
  1.6 0.0 copy-start.1
  1.6 1.0 %copy-done.1 = bf16[8,128,256]{2,1,0:T(8,128)(2,1)S(1)} copy-done((bf16[8,128,256]{2,1,0:T(8,128)(2,1)S(1)}, bf16[8,128,256]{2,1,0:T(8,128)(2,1)}, u32[]{:S(2)}) %copy-start.1) | copy-done | bytes 524312
  2.6 0.0 copy-start.2
  2.6 0.9 %copy-done.2 = bf16[8,64,256]{2,1,0:T(8,128)(2,1)S(1)} copy-done((bf16[8,64,256]{2,1,0:T(8,128)(2,1)S(1)}, bf16[8,64,256]{2,1,0:T(8,128)(2,1)}, u32[]{:S(2)}) %copy-start.2) | copy-done | bytes 262168
  3.6 0.0 copy-start.3
  3.6 0.7 copy-done.3
  4.3 0.0 copy-start.4
  4.3 0.7 copy-done.4
  4.9 70.8 %shard_map.55 = bf16[8,128,256]{2,1,0:T(8,128)(2,1)S(1)} custom-call(s32[8]{0:T(128)S(1)} %copy-done.4, s32[8,8]{1,0:T(8,128)S(1)} %copy-done.3, bf16[8,128,256]{2,1,0:T(8,128)(2,1)S(1)} %copy-done.1, bf16[8,8,64,256]{3,2,1,0:T(8,128)(2,1)S(1)} %copy-done, bf16[8,64,256]{2,1,0:T(8,128)(2,1)S(1)} %copy-done.2), custom_call_target="tpu_custom_call" | custom-call | tf_op jit(solution)/shard_map/pallas_call | solution.py:327
  75.7 0.8 %copy.7 = bf16[8,128,256]{2,1,0:T(8,128)(2,1)} copy(bf16[8,128,256]{2,1,0:T(8,128)(2,1)S(1)} %shard_map.55) | data formatting | bytes 1048576
Async XLA Ops:
  0.0 1.6 %copy-start = (bf16[8,8,64,256]{3,2,1,0:T(8,128)(2,1)S(1)}, bf16[8,8,64,256]{3,2,1,0:T(8,128)(2,1)}, u32[]{:S(2)}) copy-start(bf16[8,8,64,256]{3,2,1,0:T(8,128)(2,1)} %off_ref.1) | copy-start | bytes 6291460
  1.6 1.0 %copy-start.1 = (bf16[8,128,256]{2,1,0:T(8,128)(2,1)S(1)}, bf16[8,128,256]{2,1,0:T(8,128)(2,1)}, u32[]{:S(2)}) copy-start(bf16[8,128,256]{2,1,0:T(8,128)(2,1)} %right_ref.1) | copy-start | bytes 1572868
  2.6 0.9 %copy-start.2 = (bf16[8,64,256]{2,1,0:T(8,128)(2,1)S(1)}, bf16[8,64,256]{2,1,0:T(8,128)(2,1)}, u32[]{:S(2)}) copy-start(bf16[8,64,256]{2,1,0:T(8,128)(2,1)} %diag_ref.1) | copy-start | bytes 786436
  3.6 0.7 copy-start.3
  4.3 0.7 copy-start.4

commit v4 on v3

--- a/solution.py
+++ b/solution.py
@@ -23,8 +23,8 @@
 
 
 def kernel(
-    n, level_ref, cols_ref, right_ref, off_ref, diag_ref, out_ref,
-    fac, fac_last, inv, win, land0, land1, land2, sol0, sol1, sol2, lvl_ref, lvl_in, lvl_s, slot, perm,
+    n, level_ref, cols_ref, right_in, off_in, diag_in, out_ref,
+    right_ref, off_ref, diag_ref, in_sem, fac, fac_last, inv, win, land0, land1, land2, sol0, sol1, sol2, sol3, lvl_ref, lvl_in, lvl_s, slot, perm,
     lvl_send, lvl_recv, lvl_sem, x_send, x_recv, c_send, c_recv, f_send, f_recv,
     w0_send, w0_recv, w1_send, w1_recv, w2_send, w2_recv,
 ):
@@ -33,6 +33,12 @@
     core = mine + 1 - 2 * lax.rem(mine, 2)
     across = lax.rem(mine + 2, 4)
 
+    fetches = [
+        pltpu.make_async_copy(src, dst, in_sem.at[i])
+        for i, (src, dst) in enumerate([(diag_in, diag_ref), (off_in, off_ref), (right_in, right_ref)])
+    ]
+    for copy in fetches:
+        copy.start()
     lvl_in[...] = jnp.zeros_like(lvl_in)
     for r in range(rows):
         lvl_ref[r:r + 1, :] = jnp.full((1, lvl_ref.shape[1]), level_ref[r], jnp.int32)
@@ -132,18 +138,22 @@
         send_c(i).wait_recv()
         send_f(i).wait_recv()
 
+    fetches[0].wait()
     for p in range(rows):
         stage_diag(p)
-        if p > 0:
-            stage_off(p)
 
     greeted = jnp.int32(2)
     for d in range(1, REACH):
         greeted += (me + d < n).astype(jnp.int32) + (me >= d).astype(jnp.int32)
     pl.semaphore_wait(barrier, greeted)
 
-    for i in range(AHEAD):
-        issue(i)
+    issue(0)
+    fetches[1].wait()
+    for p in range(1, rows):
+        stage_off(p)
+        if p < AHEAD:
+            issue(p)
+    fetches[2].wait()
 
     def send_lvl(d):
         return pltpu.make_async_remote_copy(
@@ -298,9 +308,9 @@
     serve_rest(2)
     fill(2)
 
-    o = BELOW * HELD + BASE[3] - FIRST[3]
     for p in range(FIRST[3], rows):
-        win[o + p] = solve(p, fac_last[...] if p == rows - 1 else fac[p - 1], inv[p])
+        sol3[p - FIRST[3]] = solve(p, fac_last[...] if p == rows - 1 else fac[p - 1], inv[p])
+    win[BELOW * HELD + BASE[3]:] = sol3[...]
     for r in range(rows):
         out_ref[r] = win[slot[BELOW * rows + r]]
 
@@ -320,6 +330,7 @@
     samples = right_side.shape[1]
     vmem = pl.BlockSpec(memory_space=pltpu.VMEM)
     smem = pl.BlockSpec(memory_space=pltpu.SMEM)
+    anywhere = pl.BlockSpec(memory_space=pl.ANY)
     tile = (samples, bs)
     counts = COUNTS
     items = rows + 2
@@ -327,9 +338,13 @@
     return pl.pallas_call(
         functools.partial(kernel, n),
         out_shape=jax.ShapeDtypeStruct(right_side.shape, jnp.bfloat16),
-        in_specs=[smem, smem, vmem, vmem, vmem],
+        in_specs=[smem, smem, anywhere, anywhere, anywhere],
         out_specs=vmem,
         scratch_shapes=[
+            pltpu.VMEM(right_side.shape, jnp.bfloat16),
+            pltpu.VMEM(off_blocks.shape, jnp.bfloat16),
+            pltpu.VMEM(diag_inverse.shape, jnp.bfloat16),
+            dma((3,)),
             pltpu.VMEM((rows - 2, 4 * part, kk * bs), jnp.bfloat16),
             pltpu.VMEM((4 * part, kk * bs), jnp.bfloat16),
             pltpu.VMEM((rows, 4 * part, bs), jnp.bfloat16),
@@ -340,6 +355,7 @@
             pltpu.VMEM((counts[0],) + tile, jnp.bfloat16),
             pltpu.VMEM((counts[1],) + tile, jnp.bfloat16),
             pltpu.VMEM((counts[2],) + tile, jnp.bfloat16),
+            pltpu.VMEM((rows - FIRST[3],) + tile, jnp.bfloat16),
             pltpu.VMEM((rows, 128), jnp.int32),
             pltpu.VMEM((BELOW, rows, 128), jnp.int32),
             pltpu.SMEM((BELOW, rows, 128), jnp.int32),

time: 76.8 us -> 76.8 us (level)
  no operation moved by 1% of the time
where the time goes in v4:
time: 76.8 us; the launch traced here: 76.5 us
  Pallas kernels  70.8 us (92%)
  local copies, waits for them, and re-layouts  5.72 us (7%)
    pallas_call x1, Pallas kernels, per_device(): pl.pallas_call(functools.partial(kernel, n), out_shape=jax.ShapeDtypeStru...  70.8 us
    unnamed x11, local copies, waits for them, and re-layouts  5.72 us

profile of v4, /device:TPU:25, one launch (start us, length us, event | category | flops | bytes accessed | tf_op | source)
XLA Modules:
  0.0 76.5 jit_solution(16595887259012371059)
XLA Ops:
  0.0 0.0 copy-start
  0.0 1.6 %copy-done = bf16[8,8,64,256]{3,2,1,0:T(8,128)(2,1)S(1)} copy-done((bf16[8,8,64,256]{3,2,1,0:T(8,128)(2,1)S(1)}, bf16[8,8,64,256]{3,2,1,0:T(8,128)(2,1)}, u32[]{:S(2)}) %copy-start) | copy-done | bytes 2097176
  1.6 0.0 copy-start.1
  1.6 1.0 %copy-done.1 = bf16[8,128,256]{2,1,0:T(8,128)(2,1)S(1)} copy-done((bf16[8,128,256]{2,1,0:T(8,128)(2,1)S(1)}, bf16[8,128,256]{2,1,0:T(8,128)(2,1)}, u32[]{:S(2)}) %copy-start.1) | copy-done | bytes 524312
  2.6 0.0 copy-start.2
  2.6 0.9 %copy-done.2 = bf16[8,64,256]{2,1,0:T(8,128)(2,1)S(1)} copy-done((bf16[8,64,256]{2,1,0:T(8,128)(2,1)S(1)}, bf16[8,64,256]{2,1,0:T(8,128)(2,1)}, u32[]{:S(2)}) %copy-start.2) | copy-done | bytes 262168
  3.6 0.0 copy-start.3
  3.6 0.7 copy-done.3
  4.3 0.0 copy-start.4
  4.3 0.7 copy-done.4
  4.9 70.8 %shard_map.55 = bf16[8,128,256]{2,1,0:T(8,128)(2,1)S(1)} custom-call(s32[8]{0:T(128)S(1)} %copy-done.4, s32[8,8]{1,0:T(8,128)S(1)} %copy-done.3, bf16[8,128,256]{2,1,0:T(8,128)(2,1)S(1)} %copy-done.1, bf16[8,8,64,256]{3,2,1,0:T(8,128)(2,1)S(1)} %copy-done, bf16[8,64,256]{2,1,0:T(8,128)(2,1)S(1)} %copy-done.2), custom_call_target="tpu_custom_call" | custom-call | tf_op jit(solution)/shard_map/pallas_call | solution.py:338
  75.7 0.8 %copy.7 = bf16[8,128,256]{2,1,0:T(8,128)(2,1)} copy(bf16[8,128,256]{2,1,0:T(8,128)(2,1)S(1)} %shard_map.55) | data formatting | bytes 1048576
Async XLA Ops:
  0.0 1.6 %copy-start = (bf16[8,8,64,256]{3,2,1,0:T(8,128)(2,1)S(1)}, bf16[8,8,64,256]{3,2,1,0:T(8,128)(2,1)}, u32[]{:S(2)}) copy-start(bf16[8,8,64,256]{3,2,1,0:T(8,128)(2,1)} %off_in.1) | copy-start | bytes 6291460
  1.6 1.0 %copy-start.1 = (bf16[8,128,256]{2,1,0:T(8,128)(2,1)S(1)}, bf16[8,128,256]{2,1,0:T(8,128)(2,1)}, u32[]{:S(2)}) copy-start(bf16[8,128,256]{2,1,0:T(8,128)(2,1)} %right_in.1) | copy-start | bytes 1572868
  2.6 0.9 %copy-start.2 = (bf16[8,64,256]{2,1,0:T(8,128)(2,1)S(1)}, bf16[8,64,256]{2,1,0:T(8,128)(2,1)}, u32[]{:S(2)}) copy-start(bf16[8,64,256]{2,1,0:T(8,128)(2,1)} %diag_in.1) | copy-start | bytes 786436
  3.6 0.7 copy-start.3
  4.3 0.7 copy-start.4

commit v5 on v4

--- a/solution.py
+++ b/solution.py
@@ -15,7 +15,7 @@
 COUNTS = (4, 5, 4)
 BASE = (0, 4, 9, 13)
 HELD = 13
-AHEAD = 3
+AHEAD = 5
 
 
 def nt(a, b):
@@ -149,10 +149,15 @@
 
     issue(0)
     fetches[1].wait()
-    for p in range(1, rows):
+    staged = 0
+    for i in range(1, AHEAD):
+        kind, at = items[i]
+        if kind == "o":
+            stage_off(at)
+            staged = at
+        issue(i)
+    for p in range(staged + 1, rows):
         stage_off(p)
-        if p < AHEAD:
-            issue(p)
     fetches[2].wait()
 
     def send_lvl(d):
@@ -330,7 +335,7 @@
     samples = right_side.shape[1]
     vmem = pl.BlockSpec(memory_space=pltpu.VMEM)
     smem = pl.BlockSpec(memory_space=pltpu.SMEM)
-    anywhere = pl.BlockSpec(memory_space=pl.ANY)
+    anywhere = pl.BlockSpec(memory_space=pltpu.HBM)
     tile = (samples, bs)
     counts = COUNTS
     items = rows + 2
@@ -368,7 +373,7 @@
             dma((counts[2], 4)), dma((counts[2], BELOW)),
         ],
         compiler_params=pltpu.CompilerParams(
-            collective_id=0, has_side_effects=True, vmem_limit_bytes=48 * 2 ** 20),
+            collective_id=0, has_side_effects=True, vmem_limit_bytes=62 * 2 ** 20),
     )(
         block_level, block_columns, right_side, off_blocks, diag_inverse,
     )

time: 76.8 us -> 73.6 us (0.958)
  local copies, waits for them, and re-layouts: 5.72 us -> 1.87 us
    unnamed x11 -> x1, local copies, waits for them, and re-layouts: 5.72 us -> 1.87 us
where the time goes in v5:
time: 73.6 us; the launch traced here: 73.4 us
  Pallas kernels  71.5 us (97%)
  local copies, waits for them, and re-layouts  1.87 us (3%)
    pallas_call x1, Pallas kernels, per_device(): pl.pallas_call(functools.partial(kernel, n), out_shape=jax.ShapeDtypeStru...  71.5 us
    unnamed x1, local copies, waits for them, and re-layouts  1.87 us

profile of v5, /device:TPU:25, one launch (start us, length us, event | category | flops | bytes accessed | tf_op | source)
XLA Modules:
  0.0 73.4 jit_solution(12103887653879031831)
XLA Ops:
  0.0 71.5 %shard_map.55 = bf16[8,128,256]{2,1,0:T(8,128)(2,1)} custom-call(s32[8]{0:T(128)} %level_ref.1, s32[8,8]{1,0:T(8,128)} %cols_ref.1, bf16[8,128,256]{2,1,0:T(8,128)(2,1)} %right_in.1, bf16[8,8,64,256]{3,2,1,0:T(8,128)(2,1)} %off_in.1, bf16[8,64,256]{2,1,0:T(8,128)(2,1)} %diag_in.1), custom_call_target="tpu_custom_call" | custom-call | tf_op jit(solution)/shard_map/pallas_call | solution.py:343
  71.5 1.9 %copy.7 = bf16[8,128,256]{2,1,0:T(8,128)(2,1)} copy(bf16[8,128,256]{2,1,0:T(8,128)(2,1)} %shard_map.55) | data formatting | bytes 1048576

commit v6 on v5

--- a/solution.py
+++ b/solution.py
@@ -18,13 +18,13 @@
 AHEAD = 5
 
 
-def nt(a, b):
-    return lax.dot_general(a, b, (((1,), (1,)), ((), ())), preferred_element_type=jnp.float32)
+def dot(a, b):
+    return jnp.dot(a, b, preferred_element_type=jnp.float32)
 
 
 def kernel(
     n, level_ref, cols_ref, right_in, off_in, diag_in, out_ref,
-    right_ref, off_ref, diag_ref, in_sem, fac, fac_last, inv, win, land0, land1, land2, sol0, sol1, sol2, sol3, lvl_ref, lvl_in, lvl_s, slot, perm,
+    right_ref, off_ref, diag_ref, turned, in_sem, fac, fac_last, inv, win, land0, land1, land2, sol0, sol1, sol2, sol3, lvl_ref, lvl_in, lvl_s, slot, perm,
     lvl_send, lvl_recv, lvl_sem, x_send, x_recv, c_send, c_recv, f_send, f_recv,
     w0_send, w0_recv, w1_send, w1_recv, w2_send, w2_recv,
 ):
@@ -159,6 +159,8 @@
     for p in range(staged + 1, rows):
         stage_off(p)
     fetches[2].wait()
+    for r in range(rows):
+        turned[r] = right_ref[r].astype(jnp.float32).T
 
     def send_lvl(d):
         return pltpu.make_async_remote_copy(
@@ -255,7 +257,7 @@
     at_item = {p: items.index(("o", p)) for p in range(1, rows)}
     arrive(0)
     for p in range(half):
-        sol0[p] = nt(right_ref[where[p]], inv[p]).astype(jnp.bfloat16)
+        sol0[p] = dot(inv[p], turned[where[p]].astype(jnp.bfloat16)).astype(jnp.bfloat16)
         own_hops(0, p, start)
 
     each_down(lambda d: send_lvl(d).wait_recv())
@@ -271,9 +273,9 @@
         for k in range(kk):
             at = cols_ref[row, k] - (me - BELOW) * rows
             taken.append(win[slot[jnp.clip(at, 0, REACH * rows - 1)]])
-        contribution = nt(jnp.concatenate(taken, axis=1), factor)
-        residue = (right_ref[row].astype(jnp.float32) - contribution).astype(jnp.bfloat16)
-        return nt(residue, inverse).astype(jnp.bfloat16)
+        contribution = dot(factor, jnp.concatenate(taken, axis=0))
+        residue = (turned[row] - contribution).astype(jnp.bfloat16)
+        return dot(inverse, residue).astype(jnp.bfloat16)
 
     def fill(v):
         for d in range(1, REACH):
@@ -336,19 +338,20 @@
     vmem = pl.BlockSpec(memory_space=pltpu.VMEM)
     smem = pl.BlockSpec(memory_space=pltpu.SMEM)
     anywhere = pl.BlockSpec(memory_space=pltpu.HBM)
-    tile = (samples, bs)
+    tile = (bs, samples)
     counts = COUNTS
     items = rows + 2
     dma = pltpu.SemaphoreType.DMA
-    return pl.pallas_call(
+    answer = pl.pallas_call(
         functools.partial(kernel, n),
-        out_shape=jax.ShapeDtypeStruct(right_side.shape, jnp.bfloat16),
+        out_shape=jax.ShapeDtypeStruct((rows,) + tile, jnp.bfloat16),
         in_specs=[smem, smem, anywhere, anywhere, anywhere],
         out_specs=vmem,
         scratch_shapes=[
             pltpu.VMEM(right_side.shape, jnp.bfloat16),
             pltpu.VMEM(off_blocks.shape, jnp.bfloat16),
             pltpu.VMEM(diag_inverse.shape, jnp.bfloat16),
+            pltpu.VMEM((rows,) + tile, jnp.float32),
             dma((3,)),
             pltpu.VMEM((rows - 2, 4 * part, kk * bs), jnp.bfloat16),
             pltpu.VMEM((4 * part, kk * bs), jnp.bfloat16),
@@ -377,6 +380,7 @@
     )(
         block_level, block_columns, right_side, off_blocks, diag_inverse,
     )
+    return jnp.swapaxes(answer, 1, 2)
 
 
 def solution(mesh):

time: 73.6 us -> 72.6 us (0.986)
  Pallas kernels: 71.5 us -> 70.4 us
    transpose x0 -> x1, local copies, waits for them, and re-layouts: none -> 2.04 us  [per_device(): return jnp.swapaxes(answer, 1, 2)]
    unnamed x1 -> x0, local copies, waits for them, and re-layouts: 1.87 us -> none
    pallas_call x1, Pallas kernels: 71.5 us -> 70.4 us  [per_device(): pl.pallas_call(functools.partial(kernel, n), out_shape=jax.ShapeDtypeStru...]
where the time goes in v6:
time: 72.6 us; the launch traced here: 72.4 us
  Pallas kernels  70.4 us (97%)
  local copies, waits for them, and re-layouts  2.04 us (3%)
    pallas_call x1, Pallas kernels, per_device(): pl.pallas_call(functools.partial(kernel, n), out_shape=jax.ShapeDtypeStru...  70.4 us
    transpose x1, local copies, waits for them, and re-layouts, per_device(): return jnp.swapaxes(answer, 1, 2)  2.04 us

profile of v6, /device:TPU:25, one launch (start us, length us, event | category | flops | bytes accessed | tf_op | source)
XLA Modules:
  0.0 72.4 jit_solution(57817413136676304)
XLA Ops:
  0.0 70.4 %shard_map.55 = bf16[8,256,128]{2,1,0:T(8,128)(2,1)} custom-call(s32[8]{0:T(128)} %level_ref.1, s32[8,8]{1,0:T(8,128)} %cols_ref.1, bf16[8,128,256]{2,1,0:T(8,128)(2,1)} %right_in.1, bf16[8,8,64,256]{3,2,1,0:T(8,128)(2,1)} %off_in.1, bf16[8,64,256]{2,1,0:T(8,128)(2,1)} %diag_in.1), custom_call_target="tpu_custom_call" | custom-call | tf_op jit(solution)/shard_map/pallas_call | solution.py:345
  70.4 2.0 %copy.6 = bf16[8,128,256]{2,1,0:T(8,128)(2,1)} copy(bf16[8,128,256]{1,2,0:T(8,128)(2,1)} %bitcast.1) | data formatting | bytes 1048576 | tf_op jit(solution)/shard_map/transpose | solution.py:383

commit v7 on v6

--- a/solution.py
+++ b/solution.py
@@ -16,6 +16,7 @@
 BASE = (0, 4, 9, 13)
 HELD = 13
 AHEAD = 5
+SPLIT = 2
 
 
 def dot(a, b):
@@ -241,24 +242,44 @@
         def _():
             landed(v, i, 3)
 
+    def legs(leg, v, first, last):
+        for i in range(SPLIT * max(first, 0), SPLIT * max(last, 0)):
+            leg(v, i)
+
     def serve(v, i):
-        count = sols[v].shape[0]
-        for leg, late in ((first_leg, 1), (second_leg, 2), (third_leg, 3)):
-            if 0 <= i - late < count:
-                leg(v, i - late)
+        legs(first_leg, v, i - 1, i)
+        legs(second_leg, v, i - 2, i - 1)
+        legs(third_leg, v, i - 3, i - 2)
 
     def serve_rest(v):
-        count = sols[v].shape[0]
-        for i in range(count, count + 3):
-            serve(v, i)
+        count = COUNTS[v]
+        legs(second_leg, v, count - 2, count - 1)
+        legs(first_leg, v, count - 1, count)
+        legs(second_leg, v, count - 1, count)
+        legs(third_leg, v, count - 3, count)
+
+    def serve_all(v, between=None):
+        count = SPLIT * COUNTS[v]
+        for i in range(count + SPLIT):
+            if i < count:
+                first_leg(v, i)
+            if i >= SPLIT:
+                second_leg(v, i - SPLIT)
+        if between is not None:
+            between()
+        legs(third_leg, v, 0, COUNTS[v])
+
+    def put(v, i, block):
+        sols[v][SPLIT * i:SPLIT * (i + 1)] = block.reshape((SPLIT,) + sols[v].shape[1:])
+        for j in range(SPLIT * i, SPLIT * (i + 1)):
+            own_hops(v, j, start)
 
     each_up(lambda d: send_lvl(d).start())
 
     at_item = {p: items.index(("o", p)) for p in range(1, rows)}
     arrive(0)
     for p in range(half):
-        sol0[p] = dot(inv[p], turned[where[p]].astype(jnp.bfloat16)).astype(jnp.bfloat16)
-        own_hops(0, p, start)
+        put(0, p, dot(inv[p], turned[where[p]].astype(jnp.bfloat16)).astype(jnp.bfloat16))
 
     each_down(lambda d: send_lvl(d).wait_recv())
     fetch = pltpu.make_async_copy(lvl_in, lvl_s, lvl_sem)
@@ -280,15 +301,12 @@
     def fill(v):
         for d in range(1, REACH):
             o = (BELOW - d) * HELD + BASE[v]
-            win[o:o + COUNTS[v]] = lands[v][BELOW - d]
+            win[o:o + COUNTS[v]] = lands[v][BELOW - d].reshape((COUNTS[v],) + win.shape[1:])
         o = BELOW * HELD + BASE[v]
-        win[o:o + COUNTS[v]] = sols[v][...]
+        win[o:o + COUNTS[v]] = sols[v][...].reshape((COUNTS[v],) + win.shape[1:])
 
     arrive(at_item[1])
-    for i in range(half):
-        serve(0, i)
-    arrive(at_item[2])
-    serve_rest(0)
+    serve_all(0, lambda: arrive(at_item[2]))
     fill(0)
 
     for p in range(FIRST[1], LAST[1] + 1):
@@ -297,8 +315,7 @@
         if p > 2:
             arrive(at_item[p])
         i = p - FIRST[1]
-        sol1[i] = solve(p, fac[p - 1], inv[p])
-        own_hops(1, i, start)
+        put(1, i, solve(p, fac[p - 1], inv[p]))
         serve(1, i)
     serve_rest(1)
     fill(1)
@@ -308,11 +325,8 @@
         arrive(at_item[p])
     for i in range(COUNTS[2]):
         p = jnp.clip(lower2 + i, FIRST[2], LAST[2])
-        sol2[i] = solve(p, fac[p - 1], inv[p])
-        own_hops(2, i, start)
-        serve(2, i)
-    arrive(at_item[rows - 1])
-    serve_rest(2)
+        put(2, i, solve(p, fac[p - 1], inv[p]))
+    serve_all(2, lambda: arrive(at_item[rows - 1]))
     fill(2)
 
     for p in range(FIRST[3], rows):
@@ -327,7 +341,7 @@
 
     each_up(lambda d: send_lvl(d).wait_send())
     for v in range(BELOW):
-        for i in range(sols[v].shape[0]):
+        for i in range(SPLIT * COUNTS[v]):
             for hops in (own_hops, side_hops, up_hops):
                 hops(v, i, lambda copy: copy.wait_send())
 
@@ -339,7 +353,8 @@
     smem = pl.BlockSpec(memory_space=pltpu.SMEM)
     anywhere = pl.BlockSpec(memory_space=pltpu.HBM)
     tile = (bs, samples)
-    counts = COUNTS
+    sent = (bs // SPLIT, samples)
+    counts = [SPLIT * count for count in COUNTS]
     items = rows + 2
     dma = pltpu.SemaphoreType.DMA
     answer = pl.pallas_call(
@@ -357,12 +372,12 @@
             pltpu.VMEM((4 * part, kk * bs), jnp.bfloat16),
             pltpu.VMEM((rows, 4 * part, bs), jnp.bfloat16),
             pltpu.VMEM((REACH * HELD + rows - FIRST[3],) + tile, jnp.bfloat16),
-            pltpu.VMEM((BELOW, counts[0]) + tile, jnp.bfloat16),
-            pltpu.VMEM((BELOW, counts[1]) + tile, jnp.bfloat16),
-            pltpu.VMEM((BELOW, counts[2]) + tile, jnp.bfloat16),
-            pltpu.VMEM((counts[0],) + tile, jnp.bfloat16),
-            pltpu.VMEM((counts[1],) + tile, jnp.bfloat16),
-            pltpu.VMEM((counts[2],) + tile, jnp.bfloat16),
+            pltpu.VMEM((BELOW, counts[0]) + sent, jnp.bfloat16),
+            pltpu.VMEM((BELOW, counts[1]) + sent, jnp.bfloat16),
+            pltpu.VMEM((BELOW, counts[2]) + sent, jnp.bfloat16),
+            pltpu.VMEM((counts[0],) + sent, jnp.bfloat16),
+            pltpu.VMEM((counts[1],) + sent, jnp.bfloat16),
+            pltpu.VMEM((counts[2],) + sent, jnp.bfloat16),
             pltpu.VMEM((rows - FIRST[3],) + tile, jnp.bfloat16),
             pltpu.VMEM((rows, 128), jnp.int32),
             pltpu.VMEM((BELOW, rows, 128), jnp.int32),

time: 72.6 us -> 71.8 us (0.989)
  Pallas kernels: 70.4 us -> 69.3 us
    pallas_call x1, Pallas kernels: 70.4 us -> 69.3 us  [per_device(): pl.pallas_call(functools.partial(kernel, n), out_shape=jax.ShapeDtypeStru...]
where the time goes in v7:
time: 71.8 us; the launch traced here: 71.3 us
  Pallas kernels  69.3 us (97%)
  local copies, waits for them, and re-layouts  2.04 us (3%)
    pallas_call x1, Pallas kernels, per_device(): pl.pallas_call(functools.partial(kernel, n), out_shape=jax.ShapeDtypeStru...  69.3 us
    transpose x1, local copies, waits for them, and re-layouts, per_device(): return jnp.swapaxes(answer, 1, 2)  2.04 us

profile of v7, /device:TPU:25, one launch (start us, length us, event | category | flops | bytes accessed | tf_op | source)
XLA Modules:
  0.0 71.3 jit_solution(12782014782007191264)
XLA Ops:
  0.0 69.3 %shard_map.55 = bf16[8,256,128]{2,1,0:T(8,128)(2,1)} custom-call(s32[8]{0:T(128)} %level_ref.1, s32[8,8]{1,0:T(8,128)} %cols_ref.1, bf16[8,128,256]{2,1,0:T(8,128)(2,1)} %right_in.1, bf16[8,8,64,256]{3,2,1,0:T(8,128)(2,1)} %off_in.1, bf16[8,64,256]{2,1,0:T(8,128)(2,1)} %diag_in.1), custom_call_target="tpu_custom_call" | custom-call | tf_op jit(solution)/shard_map/pallas_call | solution.py:360
  69.3 2.0 %copy.6 = bf16[8,128,256]{2,1,0:T(8,128)(2,1)} copy(bf16[8,128,256]{1,2,0:T(8,128)(2,1)} %bitcast.1) | data formatting | bytes 1048576 | tf_op jit(solution)/shard_map/transpose | solution.py:398

commit v8 on v7

--- a/solution.py
+++ b/solution.py
@@ -16,7 +16,7 @@
 BASE = (0, 4, 9, 13)
 HELD = 13
 AHEAD = 5
-SPLIT = 2
+SPLIT = 4
 
 
 def dot(a, b):
@@ -209,16 +209,19 @@
             what(hop(v, i, OWN_SIDE, me + 1, 1))
 
     def side_hops(v, i, what):
-        @pl.when(even & (me >= 2))
-        def _():
-            what(hop(v, i, PASS_SIDE, me + 1, 3))
+        if i % 2 == 0:
+            @pl.when(even & (me >= 2))
+            def _():
+                what(hop(v, i, PASS_SIDE, me + 1, 3))
 
         @pl.when(odd & (me >= 2))
         def _():
             what(hop(v, i, PASS_SIDE, me - 1, 1))
 
     def up_hops(v, i, what):
-        @pl.when(even & (me >= 2) & (me + 2 < n))
+        passes = even & (me >= 2) if i % 2 == 0 else me >= 1
+
+        @pl.when(passes & (me + 2 < n))
         def _():
             what(hop(v, i, PASS_UP, me + 2, 3))
 

time: 71.8 us -> 73.2 us (1.019)
  Pallas kernels: 69.3 us -> 70.7 us
    pallas_call x1, Pallas kernels: 69.3 us -> 70.7 us  [per_device(): pl.pallas_call(functools.partial(kernel, n), out_shape=jax.ShapeDtypeStru...]
where the time goes in v8:
time: 73.2 us; the launch traced here: 72.7 us
  Pallas kernels  70.7 us (97%)
  local copies, waits for them, and re-layouts  2.04 us (3%)
    pallas_call x1, Pallas kernels, per_device(): pl.pallas_call(functools.partial(kernel, n), out_shape=jax.ShapeDtypeStru...  70.7 us
    transpose x1, local copies, waits for them, and re-layouts, per_device(): return jnp.swapaxes(answer, 1, 2)  2.04 us

profile of v8, /device:TPU:25, one launch (start us, length us, event | category | flops | bytes accessed | tf_op | source)
XLA Modules:
  0.0 72.7 jit_solution(3011057272859346203)
XLA Ops:
  0.0 70.7 %shard_map.55 = bf16[8,256,128]{2,1,0:T(8,128)(2,1)} custom-call(s32[8]{0:T(128)} %level_ref.1, s32[8,8]{1,0:T(8,128)} %cols_ref.1, bf16[8,128,256]{2,1,0:T(8,128)(2,1)} %right_in.1, bf16[8,8,64,256]{3,2,1,0:T(8,128)(2,1)} %off_in.1, bf16[8,64,256]{2,1,0:T(8,128)(2,1)} %diag_in.1), custom_call_target="tpu_custom_call" | custom-call | tf_op jit(solution)/shard_map/pallas_call | solution.py:363
  70.7 2.0 %copy.6 = bf16[8,128,256]{2,1,0:T(8,128)(2,1)} copy(bf16[8,128,256]{1,2,0:T(8,128)(2,1)} %bitcast.1) | data formatting | bytes 1048576 | tf_op jit(solution)/shard_map/transpose | solution.py:401
